TPU v7x, 768 devices: a whole 4x8x12 slice. The times are simulated.
768 devices in a mesh: table: 48 (over z, x), col: 16 (over y, core).
Axes of the slice: x: 4, y: 8, z: 12, core: 2. Of those that a mesh axis runs over, the one named last changes fastest.
Arguments:
- pooled_grad: bfloat16 [96, 512, 12288], P(None, 'col', 'table'), may hold values from -2.7 to 2.7
- row_ids: int32 [96, 4, 12288], P(None, None, 'table'), may hold values from 0 to 1023
- lengths: int32 [96, 12288], P(None, 'table'), may hold values from 1 to 4
- feature_order: int32 [96], replicated, may hold values from 0 to 95, each once
- weights: float32 [96, 512, 1024], P('table', 'col'), may hold values from -3 to 3
- state: float32 [96, 1024], P('table'), may hold values from 0.1 to 10
Outputs:
- new_weights: float32 [96, 512, 1024], P('table', 'col')
- new_state: float32 [96, 1024], P('table')
All inputs are finite; a program needn't handle non-finite values.
Results may differ from a plain program's by a relative error of at most 0.0003.
Values may be sent and summed in bfloat16 or wider, within the bound.
A program may use at most 32 MiB of HBM per device.

v0:
```python
import math

import jax
import jax.numpy as jnp
from jax import lax
from jax.sharding import PartitionSpec as P

D = 512


def slot_rows(slot_ids, slot_grad, row_count):
    sample_total = slot_ids.shape[1]
    block_size = math.gcd(sample_total, 2048)
    columns = lax.broadcasted_iota(jnp.int32, (1, row_count), 1)

    def advance(running, offset):
        ids_block = lax.dynamic_slice_in_dim(slot_ids, offset, block_size, 1)
        grad_block = lax.dynamic_slice_in_dim(slot_grad, offset, block_size, 1)
        counts = jnp.zeros((block_size, row_count), jnp.bfloat16)
        for place in range(slot_ids.shape[0]):
            counts = counts + (ids_block[place][:, None] == columns).astype(jnp.bfloat16)
        return (running + jnp.dot(grad_block, counts, preferred_element_type=jnp.float32), None)

    offsets = jnp.arange(sample_total // block_size, dtype=jnp.int32) * block_size
    initial = jnp.zeros((slot_grad.shape[0], row_count), jnp.float32)
    summed, _ = lax.scan(advance, initial, offsets)
    return summed


def body(pooled_grad, row_ids, lengths, feature_order, weights, state):
    position = lax.broadcasted_iota(jnp.int32, row_ids.shape, 1)
    live_ids = jnp.where(position < lengths[:, None, :], row_ids, -1)
    live_ids = jnp.take(live_ids, feature_order, axis=0)
    ordered = jnp.take(pooled_grad, feature_order, axis=0)
    owned_ids = lax.all_to_all(live_ids, "table", split_axis=0, concat_axis=2, tiled=True)
    owned_grad = lax.all_to_all(ordered, "table", split_axis=0, concat_axis=2, tiled=True)
    row_count = weights.shape[2]

    def one_slot(paired):
        return slot_rows(paired[0], paired[1], row_count)

    row_grad = lax.map(one_slot, (owned_ids, owned_grad))
    squares = jnp.sum(row_grad * row_grad, axis=1)
    summed = lax.psum(squares, "col")
    new_state = state + summed / D
    new_weights = weights - 0.3 * row_grad / jnp.sqrt(new_state)[:, None, :]
    return (new_weights, new_state)


def solution(mesh):
    placed = (
        P(None, "col", "table"),
        P(None, None, "table"),
        P(None, "table"),
        P(),
        P("table", "col", None),
        P("table", None),
    )
    return jax.shard_map(
        body,
        mesh=mesh,
        in_specs=placed,
        out_specs=(P("table", "col", None), P("table", None)),
        check_vma=False,
    )
```

profile of v0, /device:TPU:1, one launch (start us, length us, event | category | flops | bytes accessed | tf_op | source)
XLA Modules:
  0.0 234.6 jit_solution(13434397824118337678)
XLA Ops:
  0.6 0.0 copy-start
  0.6 0.8 compare_select_fusion
  1.4 0.7 compare_and_fusion
  2.1 1.1 fusion.23
  3.2 0.8 gather_fusion
  4.0 0.9 broadcast_select_fusion.1
  5.0 18.8 %all-to-all-start = ((s32[96,4,256]{2,1,0:T(4,128)}), s32[96,4,256]{2,1,0:T(4,128)S(1)}, u32[]{:S(2)}, u32[]{:S(2)}) async-start(s32[96,4,256]{2,1,0:T(4,128)} %broadcast_select_fusion.1), calls=%async_computation | async-start | bytes 786432 | tf_op jit(solution)/shard_map/all_to_all | solution.py:35
  23.8 0.0 copy-done
  23.8 1.9 gather_fusion.1
  25.7 2.8 %broadcast_select_fusion = bf16[96,32,256]{2,1,0:T(8,128)(2,1)} fusion(bf16[96,32,256]{2,1,0:T(8,128)(2,1)} %gather_fusion.1, pred[96]{0:T(512)(128)(4,1)S(1)} %compare_and_fusion), kind=kLoop, calls=%fused_computation.28 | loop fusion | flops 786432 | bytes 3145824 | tf_op jit(solution)/shard_map/jit(_take)/select_n | solution.py:34
  28.5 15.3 %all-to-all-done = s32[96,4,256]{2,1,0:T(4,128)S(1)} async-done(((s32[96,4,256]{2,1,0:T(4,128)}), s32[96,4,256]{2,1,0:T(4,128)S(1)}, u32[]{:S(2)}, u32[]{:S(2)}) %all-to-all-start) | async-done | bytes 393248 | tf_op jit(solution)/shard_map/all_to_all | solution.py:35
  43.8 6.2 %all-to-all-start.1 = ((bf16[96,32,256]{2,1,0:T(8,128)(2,1)}), bf16[96,32,256]{2,1,0:T(8,128)(2,1)}, u32[]{:S(2)}, u32[]{:S(2)}) async-start(bf16[96,32,256]{2,1,0:T(8,128)(2,1)} %broadcast_select_fusion), calls=%async_computation.1 | async-start | bytes 3145728 | tf_op jit(solution)/shard_map/all_to_all | solution.py:36
  50.1 0.1 copy.13
  50.2 0.2 all_to_all.29
  50.4 54.1 %all-to-all-done.1 = bf16[96,32,256]{2,1,0:T(8,128)(2,1)} async-done(((bf16[96,32,256]{2,1,0:T(8,128)(2,1)}), bf16[96,32,256]{2,1,0:T(8,128)(2,1)}, u32[]{:S(2)}, u32[]{:S(2)}) %all-to-all-start.1) | async-done | bytes 1572896 | tf_op jit(solution)/shard_map/all_to_all | solution.py:36
  104.5 3.4 %copy.12 = bf16[48,2,32,256]{3,0,2,1:T(8,128)(2,1)} copy(bf16[48,2,32,256]{3,2,1,0:T(8,128)(2,1)} %bitcast.5) | data formatting | bytes 3145728 | tf_op jit(solution)/shard_map/all_to_all | solution.py:36
  108.0 3.6 %all_to_all.33 = bf16[2,32,12288]{2,1,0:T(8,128)(2,1)} reshape(bf16[2,32,48,256]{3,2,1,0:T(8,128)(2,1)} %bitcast.39) | data formatting | bytes 3145728 | tf_op jit(solution)/shard_map/all_to_all | solution.py:36
  111.6 0.0 copy-start.1
  111.6 91.8 %while.23 = (s32[]{:T(128)}, f32[2,32,1024]{2,1,0:T(8,128)S(1)}, s32[2,4,12288]{2,1,0:T(4,128)S(1)}, bf16[2,32,12288]{2,1,0:T(8,128)(2,1)}, s32[]{:T(128)}, /*in...) while((s32[]{:T(128)}, f32[2,32,1024]{2,1,0:T(8,128)S(1)}, ...), condition=%wide.region_3.4_spmd, body=%wide.region_0.0_spmd.sunk | while | flops 167837696 | bytes 2720214 | solution.py:42
  111.6 1.2 dynamic-slice_bitcast_fusion.4
  112.8 44.6 %while.24 = (s32[]{:T(128)}, f32[32,1024]{1,0:T(8,128)S(1)}, s32[6]{0:T(128)S(1)}, bf16[32,12288]{1,0:T(8,128)(2,1)S(1)}, s32[4,12288]{1,0:T(4,128)S(1)}, /*inde...) while((s32[]{:T(128)}, f32[32,1024]{1,0:T(8,128)S(1)}, ...), condition=%wide.region_2.2_spmd.clone.clone, body=%wide.region_1.1_spmd.clone.clone.sunk | while | flops 167837696 | bytes 491741 | solution.py:26
  112.8 0.7 dynamic_slice.35
  115.6 0.1 constant_dynamic-slice_fusion.2
  115.7 4.5 %fusion.30 = f32[32,1024]{1,0:T(8,128)S(1)} fusion(s32[2048]{0:T(1024)S(1)} %bitcast.43, s32[2048]{0:T(1024)S(1)} %bitcast.41, s32[2048]{0:T(1024)S(1)} %bitcast.42, s32[2048]{0:T(1024)S(1)} %bitcast.40, f32[32,1024]{1,0:T(8,128)S(1)} %get-tuple-element.217, bf16[32,12288]{1,0:T(8,128)(2,1)S(1)} %get-tuple-element.230, s32[]{:T(128)S(6)} %select_n.36, ...), kind=kOutput, calls=%fused_computation.19.clone.1 | convolution fusion | flops 167837696 | bytes 425989 | tf_op jit(solution)/shard_map/while/body/eval_jaxpr/while/body/eval_jaxpr/dot_general | solution.py:22
  120.3 0.7 dynamic_slice.35
  123.0 0.1 constant_dynamic-slice_fusion.2
  123.2 4.5 %fusion.30 = f32[32,1024]{1,0:T(8,128)S(1)} fusion(s32[2048]{0:T(1024)S(1)} %bitcast.43, s32[2048]{0:T(1024)S(1)} %bitcast.41, s32[2048]{0:T(1024)S(1)} %bitcast.42, s32[2048]{0:T(1024)S(1)} %bitcast.40, f32[32,1024]{1,0:T(8,128)S(1)} %get-tuple-element.217, bf16[32,12288]{1,0:T(8,128)(2,1)S(1)} %get-tuple-element.230, s32[]{:T(128)S(6)} %select_n.36, ...), kind=kOutput, calls=%fused_computation.19.clone.1 | convolution fusion | flops 167837696 | bytes 425989 | tf_op jit(solution)/shard_map/while/body/eval_jaxpr/while/body/eval_jaxpr/dot_general | solution.py:22
  127.7 0.7 dynamic_slice.35
  130.4 0.1 constant_dynamic-slice_fusion.2
  130.6 4.5 %fusion.30 = f32[32,1024]{1,0:T(8,128)S(1)} fusion(s32[2048]{0:T(1024)S(1)} %bitcast.43, s32[2048]{0:T(1024)S(1)} %bitcast.41, s32[2048]{0:T(1024)S(1)} %bitcast.42, s32[2048]{0:T(1024)S(1)} %bitcast.40, f32[32,1024]{1,0:T(8,128)S(1)} %get-tuple-element.217, bf16[32,12288]{1,0:T(8,128)(2,1)S(1)} %get-tuple-element.230, s32[]{:T(128)S(6)} %select_n.36, ...), kind=kOutput, calls=%fused_computation.19.clone.1 | convolution fusion | flops 167837696 | bytes 425989 | tf_op jit(solution)/shard_map/while/body/eval_jaxpr/while/body/eval_jaxpr/dot_general | solution.py:22
  135.1 0.7 dynamic_slice.35
  137.9 0.1 constant_dynamic-slice_fusion.2
  138.0 4.5 %fusion.30 = f32[32,1024]{1,0:T(8,128)S(1)} fusion(s32[2048]{0:T(1024)S(1)} %bitcast.43, s32[2048]{0:T(1024)S(1)} %bitcast.41, s32[2048]{0:T(1024)S(1)} %bitcast.42, s32[2048]{0:T(1024)S(1)} %bitcast.40, f32[32,1024]{1,0:T(8,128)S(1)} %get-tuple-element.217, bf16[32,12288]{1,0:T(8,128)(2,1)S(1)} %get-tuple-element.230, s32[]{:T(128)S(6)} %select_n.36, ...), kind=kOutput, calls=%fused_computation.19.clone.1 | convolution fusion | flops 167837696 | bytes 425989 | tf_op jit(solution)/shard_map/while/body/eval_jaxpr/while/body/eval_jaxpr/dot_general | solution.py:22
  142.6 0.7 dynamic_slice.35
  145.3 0.1 constant_dynamic-slice_fusion.2
  145.5 4.5 %fusion.30 = f32[32,1024]{1,0:T(8,128)S(1)} fusion(s32[2048]{0:T(1024)S(1)} %bitcast.43, s32[2048]{0:T(1024)S(1)} %bitcast.41, s32[2048]{0:T(1024)S(1)} %bitcast.42, s32[2048]{0:T(1024)S(1)} %bitcast.40, f32[32,1024]{1,0:T(8,128)S(1)} %get-tuple-element.217, bf16[32,12288]{1,0:T(8,128)(2,1)S(1)} %get-tuple-element.230, s32[]{:T(128)S(6)} %select_n.36, ...), kind=kOutput, calls=%fused_computation.19.clone.1 | convolution fusion | flops 167837696 | bytes 425989 | tf_op jit(solution)/shard_map/while/body/eval_jaxpr/while/body/eval_jaxpr/dot_general | solution.py:22
  150.0 0.7 dynamic_slice.35
  152.7 0.1 constant_dynamic-slice_fusion.2
  152.9 4.5 %fusion.30 = f32[32,1024]{1,0:T(8,128)S(1)} fusion(s32[2048]{0:T(1024)S(1)} %bitcast.43, s32[2048]{0:T(1024)S(1)} %bitcast.41, s32[2048]{0:T(1024)S(1)} %bitcast.42, s32[2048]{0:T(1024)S(1)} %bitcast.40, f32[32,1024]{1,0:T(8,128)S(1)} %get-tuple-element.217, bf16[32,12288]{1,0:T(8,128)(2,1)S(1)} %get-tuple-element.230, s32[]{:T(128)S(6)} %select_n.36, ...), kind=kOutput, calls=%fused_computation.19.clone.1 | convolution fusion | flops 167837696 | bytes 425989 | tf_op jit(solution)/shard_map/while/body/eval_jaxpr/while/body/eval_jaxpr/dot_general | solution.py:22
  157.5 1.2 dynamic-slice_bitcast_fusion.4
  158.7 44.6 %while.24 = (s32[]{:T(128)}, f32[32,1024]{1,0:T(8,128)S(1)}, s32[6]{0:T(128)S(1)}, bf16[32,12288]{1,0:T(8,128)(2,1)S(1)}, s32[4,12288]{1,0:T(4,128)S(1)}, /*inde...) while((s32[]{:T(128)}, f32[32,1024]{1,0:T(8,128)S(1)}, ...), condition=%wide.region_2.2_spmd.clone.clone, body=%wide.region_1.1_spmd.clone.clone.sunk | while | flops 167837696 | bytes 491741 | solution.py:26
  158.7 0.7 dynamic_slice.35
  161.5 0.1 constant_dynamic-slice_fusion.2
  161.6 4.5 %fusion.30 = f32[32,1024]{1,0:T(8,128)S(1)} fusion(s32[2048]{0:T(1024)S(1)} %bitcast.43, s32[2048]{0:T(1024)S(1)} %bitcast.41, s32[2048]{0:T(1024)S(1)} %bitcast.42, s32[2048]{0:T(1024)S(1)} %bitcast.40, f32[32,1024]{1,0:T(8,128)S(1)} %get-tuple-element.217, bf16[32,12288]{1,0:T(8,128)(2,1)S(1)} %get-tuple-element.230, s32[]{:T(128)S(6)} %select_n.36, ...), kind=kOutput, calls=%fused_computation.19.clone.1 | convolution fusion | flops 167837696 | bytes 425989 | tf_op jit(solution)/shard_map/while/body/eval_jaxpr/while/body/eval_jaxpr/dot_general | solution.py:22
  166.2 0.7 dynamic_slice.35
  168.9 0.1 constant_dynamic-slice_fusion.2
  169.1 4.5 %fusion.30 = f32[32,1024]{1,0:T(8,128)S(1)} fusion(s32[2048]{0:T(1024)S(1)} %bitcast.43, s32[2048]{0:T(1024)S(1)} %bitcast.41, s32[2048]{0:T(1024)S(1)} %bitcast.42, s32[2048]{0:T(1024)S(1)} %bitcast.40, f32[32,1024]{1,0:T(8,128)S(1)} %get-tuple-element.217, bf16[32,12288]{1,0:T(8,128)(2,1)S(1)} %get-tuple-element.230, s32[]{:T(128)S(6)} %select_n.36, ...), kind=kOutput, calls=%fused_computation.19.clone.1 | convolution fusion | flops 167837696 | bytes 425989 | tf_op jit(solution)/shard_map/while/body/eval_jaxpr/while/body/eval_jaxpr/dot_general | solution.py:22
  173.6 0.7 dynamic_slice.35
  176.3 0.1 constant_dynamic-slice_fusion.2
  176.5 4.5 %fusion.30 = f32[32,1024]{1,0:T(8,128)S(1)} fusion(s32[2048]{0:T(1024)S(1)} %bitcast.43, s32[2048]{0:T(1024)S(1)} %bitcast.41, s32[2048]{0:T(1024)S(1)} %bitcast.42, s32[2048]{0:T(1024)S(1)} %bitcast.40, f32[32,1024]{1,0:T(8,128)S(1)} %get-tuple-element.217, bf16[32,12288]{1,0:T(8,128)(2,1)S(1)} %get-tuple-element.230, s32[]{:T(128)S(6)} %select_n.36, ...), kind=kOutput, calls=%fused_computation.19.clone.1 | convolution fusion | flops 167837696 | bytes 425989 | tf_op jit(solution)/shard_map/while/body/eval_jaxpr/while/body/eval_jaxpr/dot_general | solution.py:22
  181.0 0.7 dynamic_slice.35
  183.8 0.1 constant_dynamic-slice_fusion.2
  183.9 4.5 %fusion.30 = f32[32,1024]{1,0:T(8,128)S(1)} fusion(s32[2048]{0:T(1024)S(1)} %bitcast.43, s32[2048]{0:T(1024)S(1)} %bitcast.41, s32[2048]{0:T(1024)S(1)} %bitcast.42, s32[2048]{0:T(1024)S(1)} %bitcast.40, f32[32,1024]{1,0:T(8,128)S(1)} %get-tuple-element.217, bf16[32,12288]{1,0:T(8,128)(2,1)S(1)} %get-tuple-element.230, s32[]{:T(128)S(6)} %select_n.36, ...), kind=kOutput, calls=%fused_computation.19.clone.1 | convolution fusion | flops 167837696 | bytes 425989 | tf_op jit(solution)/shard_map/while/body/eval_jaxpr/while/body/eval_jaxpr/dot_general | solution.py:22
  188.5 0.7 dynamic_slice.35
  191.2 0.1 constant_dynamic-slice_fusion.2
  191.4 4.5 %fusion.30 = f32[32,1024]{1,0:T(8,128)S(1)} fusion(s32[2048]{0:T(1024)S(1)} %bitcast.43, s32[2048]{0:T(1024)S(1)} %bitcast.41, s32[2048]{0:T(1024)S(1)} %bitcast.42, s32[2048]{0:T(1024)S(1)} %bitcast.40, f32[32,1024]{1,0:T(8,128)S(1)} %get-tuple-element.217, bf16[32,12288]{1,0:T(8,128)(2,1)S(1)} %get-tuple-element.230, s32[]{:T(128)S(6)} %select_n.36, ...), kind=kOutput, calls=%fused_computation.19.clone.1 | convolution fusion | flops 167837696 | bytes 425989 | tf_op jit(solution)/shard_map/while/body/eval_jaxpr/while/body/eval_jaxpr/dot_general | solution.py:22
  195.9 0.7 dynamic_slice.35
  198.6 0.1 constant_dynamic-slice_fusion.2
  198.8 4.5 %fusion.30 = f32[32,1024]{1,0:T(8,128)S(1)} fusion(s32[2048]{0:T(1024)S(1)} %bitcast.43, s32[2048]{0:T(1024)S(1)} %bitcast.41, s32[2048]{0:T(1024)S(1)} %bitcast.42, s32[2048]{0:T(1024)S(1)} %bitcast.40, f32[32,1024]{1,0:T(8,128)S(1)} %get-tuple-element.217, bf16[32,12288]{1,0:T(8,128)(2,1)S(1)} %get-tuple-element.230, s32[]{:T(128)S(6)} %select_n.36, ...), kind=kOutput, calls=%fused_computation.19.clone.1 | convolution fusion | flops 167837696 | bytes 425989 | tf_op jit(solution)/shard_map/while/body/eval_jaxpr/while/body/eval_jaxpr/dot_general | solution.py:22
  203.4 28.8 %psum.7 = f32[2,1024]{1,0:T(2,128)S(1)} all-reduce(f32[2,1024]{1,0:T(2,128)S(1)} %multiply_reduce_fusion), channel_id=1, replica_groups=mesh['table'=48,'col'=16] {'col'}, use_global_device_ids=true, to_apply=%region_5.6 | all-reduce | flops 2048 | bytes 16384 | tf_op jit(solution)/shard_map/psum | solution.py:44
  232.2 0.0 copy-done.1
  232.3 0.6 fusion.24
  232.9 1.7 divide_subtract_fusion
  (11 shorter events, 0.1 us)
Async XLA Ops:
  0.6 23.2 %copy-start = (bf16[96,32,256]{2,1,0:T(8,128)(2,1)S(1)}, bf16[96,32,256]{2,1,0:T(8,128)(2,1)}, u32[]{:S(2)}) copy-start(bf16[96,32,256]{2,1,0:T(8,128)(2,1)} %param.10) | copy-start | bytes 4718596
  5.0 38.9 %all-to-all-start = ((s32[96,4,256]{2,1,0:T(4,128)}), s32[96,4,256]{2,1,0:T(4,128)S(1)}, u32[]{:S(2)}, u32[]{:S(2)}) async-start(s32[96,4,256]{2,1,0:T(4,128)} %broadcast_select_fusion.1), calls=%async_computation | async-start | bytes 786432 | tf_op jit(solution)/shard_map/all_to_all | solution.py:35
  43.8 60.7 %all-to-all-start.1 = ((bf16[96,32,256]{2,1,0:T(8,128)(2,1)}), bf16[96,32,256]{2,1,0:T(8,128)(2,1)}, u32[]{:S(2)}, u32[]{:S(2)}) async-start(bf16[96,32,256]{2,1,0:T(8,128)(2,1)} %broadcast_select_fusion), calls=%async_computation.1 | async-start | bytes 3145728 | tf_op jit(solution)/shard_map/all_to_all | solution.py:36
  111.6 120.7 %copy-start.1 = (f32[2,1024]{1,0:T(2,128)S(1)}, f32[2,1024]{1,0:T(2,128)}, u32[]{:S(2)}) copy-start(f32[2,1024]{1,0:T(2,128)} %param.15) | copy-start | bytes 24580
where the time goes:
time: 235 us
  waiting for transfers between devices  69.4 us (30%)
  matrix products  54.2 us (23%)
  blocking collectives  28.8 us (12%)
  loops' own time  25.4 us (11%)
  starting transfers between devices  25.1 us (11%)
  local copies, waits for them, and re-layouts  22.3 us (9%)
  other arithmetic  8.64 us (4%)
    dot_general x12, matrix products, advance(): jnp.dot(grad_block, counts, preferred_element_type=jnp.float32)  54.2 us
    all_to_all x1, waiting for transfers between devices, body(): lax.all_to_all(ordered, 'table', split_axis=0, concat_axis=2, tiled=True)  54.1 us
    psum x1, blocking collectives, body(): summed = lax.psum(squares, 'col')  28.8 us
    another operation x2, loops' own time, slot_rows(): summed, _ = lax.scan(advance, initial, offsets)  25.3 us
    all_to_all x1, starting transfers between devices, body(): lax.all_to_all(live_ids, 'table', split_axis=0, concat_axis=2, tiled=True)  18.8 us
    all_to_all x1, waiting for transfers between devices, body(): lax.all_to_all(live_ids, 'table', split_axis=0, concat_axis=2, tiled=True)  15.3 us
    dynamic_slice x12, local copies, waits for them, and re-layouts, slot_rows(): summed, _ = lax.scan(advance, initial, offsets)  8.05 us
    all_to_all x2, local copies, waits for them, and re-layouts, body(): lax.all_to_all(ordered, 'table', split_axis=0, concat_axis=2, tiled=True)  7.02 us
  transfers between devices with their start and end apart: 2, of which 2 were waited for; matrix products, arithmetic and copies ran while one was open for 2% of the time, Pallas kernels for 0%

commit v1 on v0

v1 whole, which is shorter than its diff:
```python
import functools

import jax
import jax.numpy as jnp
from jax import lax
from jax.experimental import pallas as pl
from jax.experimental.pallas import tpu as pltpu
from jax.sharding import PartitionSpec as P

MESH = pl.DeviceIdType.MESH
LOW = 256


def kernel(
    tables, cols, width, place_count, order_ref, grad_ref, ids_ref, len_ref, w_ref, state_ref,
    new_w_ref, new_state_ref,
    send_grad, recv_grad, send_ids, all_ids, acc, squares,
    gs_sem, gr_sem, is_sem, ir_sem, cs_sem, cr_sem, qs_sem, qr_sem,
):
    t = lax.axis_index("table")
    c = lax.axis_index("col")
    slots = w_ref.shape[0]
    dim = w_ref.shape[1]
    rows = w_ref.shape[2]
    samples = grad_ref.shape[2]
    highs = rows // LOW
    across = 4 if tables % 4 == 0 else 1
    deep = tables // across
    shares = tables // cols

    def partner(step, sign):
        q = step // across
        dx = step % across
        far = (q + 1) // 2
        dz = (q % 2) * far + (1 - q % 2) * (deep - far)
        z = t // across
        x = t % across
        pz = (z + sign * dz + 2 * deep) % deep
        px = (x + sign * dx + 2 * across) % across
        return pz * across + px

    barrier = pltpu.get_barrier_semaphore()

    @pl.loop(1, tables)
    def _(step):
        pl.semaphore_signal(barrier, inc=1, device_id=(partner(step, 1), c), device_id_type=MESH)

    @pl.loop(1, cols)
    def _(step):
        pl.semaphore_signal(barrier, inc=1, device_id=(t, (c + step) % cols), device_id_type=MESH)

    place = lax.broadcasted_iota(jnp.int32, (place_count, samples), 0)

    def ids_target(share):
        return (c - t % cols + cols) % cols + cols * share

    for share in range(shares):
        target = ids_target(share)
        live = []
        for slot in range(slots):
            feature = order_ref[slots * target + slot]
            length = len_ref[pl.ds(feature, 1), :]
            live.append(jnp.where(place < length, ids_ref[feature], -1))
        send_ids[share] = jnp.concatenate(live, axis=0)

    acc[...] = jnp.zeros_like(acc)
    for slot in range(slots):
        recv_grad[t, slot] = grad_ref[order_ref[slots * t + slot]]

    pl.semaphore_wait(barrier, tables - 1 + cols - 1)

    def ids_copy(share):
        return pltpu.make_async_remote_copy(
            src_ref=send_ids.at[share],
            dst_ref=all_ids.at[c, t // cols],
            send_sem=is_sem.at[share],
            recv_sem=ir_sem.at[t // cols],
            device_id=(ids_target(share), c),
            device_id_type=MESH,
        )

    for share in range(shares):
        @pl.when(ids_target(share) == t)
        def _():
            all_ids[c, t // cols] = send_ids[share]

        @pl.when(ids_target(share) != t)
        def _():
            ids_copy(share).start()

    def grad_copy(target):
        return pltpu.make_async_remote_copy(
            src_ref=send_grad.at[target],
            dst_ref=recv_grad.at[t],
            send_sem=gs_sem.at[target],
            recv_sem=gr_sem.at[t],
            device_id=(target, c),
            device_id_type=MESH,
        )

    @pl.loop(1, tables)
    def _(step):
        target = partner(step, 1)
        for slot in range(slots):
            send_grad[target, slot] = grad_ref[order_ref[slots * target + slot]]
        grad_copy(target).start()

    def ids_arrival(share):
        return pltpu.make_async_remote_copy(
            src_ref=send_ids.at[share],
            dst_ref=all_ids.at[c, share],
            send_sem=is_sem.at[share],
            recv_sem=ir_sem.at[share],
            device_id=(ids_target(share), c),
            device_id_type=MESH,
        )

    for share in range(shares):
        @pl.when(ids_target(share) != t)
        def _():
            ids_arrival(share).wait_recv()

    def col_ids(peer):
        return pltpu.make_async_remote_copy(
            src_ref=all_ids.at[c],
            dst_ref=all_ids.at[c],
            send_sem=cs_sem.at[peer],
            recv_sem=cr_sem.at[c],
            device_id=(t, peer),
            device_id_type=MESH,
        )

    def col_ids_arrival(peer):
        return pltpu.make_async_remote_copy(
            src_ref=all_ids.at[peer],
            dst_ref=all_ids.at[peer],
            send_sem=cs_sem.at[peer],
            recv_sem=cr_sem.at[peer],
            device_id=(t, peer),
            device_id_type=MESH,
        )

    @pl.loop(1, cols)
    def _(step):
        col_ids((c + step) % cols).start()

    @pl.loop(1, cols)
    def _(step):
        col_ids_arrival((c - step + cols) % cols).wait_recv()

    low_line = lax.broadcasted_iota(jnp.int32, (LOW, samples), 0)
    zero = jnp.zeros((dim, samples), jnp.bfloat16)

    def work(source):
        block = all_ids[(source + t) % cols, source // cols]
        high = block >> 8
        low = block & (LOW - 1)
        for slot in range(slots):
            grad = recv_grad[source, slot]
            left, right = [], []
            for p in range(place_count):
                row = slot * place_count + p
                low_row = jnp.broadcast_to(low[row:row + 1], (LOW, samples))
                right.append(jnp.where(low_row == low_line, 1.0, 0.0).astype(jnp.bfloat16))
                high_row = jnp.broadcast_to(high[row:row + 1], (dim, samples))
                left.append(jnp.concatenate(
                    [grad * jnp.where(high_row == h, 1.0, 0.0).astype(jnp.bfloat16) for h in range(highs)], axis=0))
            acc[slot] += lax.dot_general(
                jnp.concatenate(left, axis=1), jnp.concatenate(right, axis=1),
                (((1,), (1,)), ((), ())), preferred_element_type=jnp.float32)

    work(t)

    @pl.loop(1, tables)
    def _(step):
        source = partner(step, -1)
        pltpu.make_async_remote_copy(
            src_ref=send_grad.at[source],
            dst_ref=recv_grad.at[source],
            send_sem=gs_sem.at[source],
            recv_sem=gr_sem.at[source],
            device_id=(source, c),
            device_id_type=MESH,
        ).wait_recv()
        work(source)

    sums = []
    for slot in range(slots):
        for h in range(highs):
            part = acc[slot, h * dim:(h + 1) * dim, :]
            sums.append(jnp.sum(part * part, axis=0, keepdims=True))
    squares[c] = jnp.concatenate(sums, axis=0)

    def square_copy(peer, owner):
        return pltpu.make_async_remote_copy(
            src_ref=squares.at[owner],
            dst_ref=squares.at[owner],
            send_sem=qs_sem.at[peer],
            recv_sem=qr_sem.at[owner],
            device_id=(t, peer),
            device_id_type=MESH,
        )

    @pl.loop(1, cols)
    def _(step):
        square_copy((c + step) % cols, c).start()

    @pl.loop(1, cols)
    def _(step):
        peer = (c - step + cols) % cols
        square_copy(peer, peer).wait_recv()

    total = squares[0]
    for peer in range(1, cols):
        total = total + squares[peer]
    full = dim * cols
    for slot in range(slots):
        for h in range(highs):
            row = slot * highs + h
            span = slice(h * LOW, (h + 1) * LOW)
            new_state = state_ref[slot:slot + 1, span] + total[row:row + 1] / full
            new_state_ref[slot:slot + 1, span] = new_state
            scale = 0.3 / jnp.sqrt(new_state)
            new_w_ref[slot, :, span] = w_ref[slot, :, span] - acc[slot, h * dim:(h + 1) * dim, :] * scale

    for share in range(shares):
        @pl.when(ids_target(share) != t)
        def _():
            ids_copy(share).wait_send()

    @pl.loop(1, cols)
    def _(step):
        peer = (c + step) % cols
        col_ids(peer).wait_send()
        square_copy(peer, c).wait_send()

    @pl.loop(1, tables)
    def _(step):
        grad_copy(partner(step, 1)).wait_send()


def solution(mesh):
    tables, cols = mesh.shape["table"], mesh.shape["col"]

    def body(pooled_grad, row_ids, lengths, feature_order, weights, state):
        features, width, samples = pooled_grad.shape
        place_count = row_ids.shape[1]
        slots, dim, rows = weights.shape
        shares = tables // cols
        vmem = pl.BlockSpec(memory_space=pltpu.VMEM)
        dma = pltpu.SemaphoreType.DMA
        return pl.pallas_call(
            functools.partial(kernel, tables, cols, width, place_count),
            out_shape=(
                jax.ShapeDtypeStruct(weights.shape, jnp.float32),
                jax.ShapeDtypeStruct(state.shape, jnp.float32),
            ),
            in_specs=[pl.BlockSpec(memory_space=pltpu.SMEM)] + [vmem] * 5,
            out_specs=(vmem, vmem),
            scratch_shapes=[
                pltpu.VMEM((tables, slots, dim, samples), jnp.bfloat16),
                pltpu.VMEM((tables, slots, dim, samples), jnp.bfloat16),
                pltpu.VMEM((shares, slots * place_count, samples), jnp.int32),
                pltpu.VMEM((cols, shares, slots * place_count, samples), jnp.int32),
                pltpu.VMEM((slots, rows // LOW * dim, LOW), jnp.float32),
                pltpu.VMEM((cols, slots * (rows // LOW), LOW), jnp.float32),
                dma((tables,)), dma((tables,)),
                dma((shares,)), dma((shares,)),
                dma((cols,)), dma((cols,)),
                dma((cols,)), dma((cols,)),
            ],
            compiler_params=pltpu.CompilerParams(
                collective_id=0, has_side_effects=True, vmem_limit_bytes=32 * 1024 * 1024
            ),
            cost_estimate=pl.CostEstimate(
                flops=4 * slots * tables * samples * rows * dim, bytes_accessed=4 * 1024 * 1024, transcendentals=0
            ),
        )(feature_order, pooled_grad, row_ids, lengths, weights, state)

    return jax.shard_map(
        body,
        mesh=mesh,
        in_specs=(
            P(None, "col", "table"),
            P(None, None, "table"),
            P(None, "table"),
            P(),
            P("table", "col", None),
            P("table", None),
        ),
        out_specs=(P("table", "col", None), P("table", None)),
        check_vma=False,
    )
```

time: 235 us -> 96.3 us (0.41)
  Pallas kernels: 0 us -> 88.4 us
  waiting for transfers between devices: 69.4 us -> 0 us
  matrix products: 54.2 us -> 0 us
  blocking collectives: 28.8 us -> 0 us
  loops' own time: 25.4 us -> 0 us
  starting transfers between devices: 25.1 us -> 0 us
  local copies, waits for them, and re-layouts: 22.3 us -> 6.89 us
  other arithmetic: 8.64 us -> 0 us
    pallas_call x0 -> x1, Pallas kernels: none -> 88.4 us  [body(): pl.pallas_call(functools.partial(kernel, tables, cols, width, place_count...]
    all_to_all x2 -> x0, waiting for transfers between devices: 69.4 us -> none  [the longest x1 54.1 us: body(): lax.all_to_all(ordered, 'table', split_axis=0, concat_axis=2, tiled=True)]
    dot_general x12 -> x0, matrix products: 54.2 us -> none  [advance(): jnp.dot(grad_block, counts, preferred_element_type=jnp.float32)]
    psum x1 -> x0, blocking collectives: 28.8 us -> none  [body(): summed = lax.psum(squares, 'col')]
    another operation x3 -> x0, loops' own time: 25.4 us -> none  [the longest x2 25.3 us: slot_rows(): summed, _ = lax.scan(advance, initial, offsets)]
    all_to_all x2 -> x0, starting transfers between devices: 25.1 us -> none  [the longest x1 18.8 us: body(): lax.all_to_all(live_ids, 'table', split_axis=0, concat_axis=2, tiled=True)]
    dynamic_slice x12 -> x0, local copies, waits for them, and re-layouts: 8.05 us -> none  [slot_rows(): summed, _ = lax.scan(advance, initial, offsets)]
    all_to_all x4 -> x0, local copies, waits for them, and re-layouts: 7.34 us -> none  [the longest x2 7.02 us: body(): lax.all_to_all(ordered, 'table', split_axis=0, concat_axis=2, tiled=True)]
  transfers between devices with their start and end apart: 2 -> 0, of which waited for: 2 -> 0; matrix products, arithmetic and copies ran while one was open for 2% -> 0% of each run, Pallas kernels for 0% -> 0%
where the time goes in v1:
time: 96.3 us; the launch traced here: 96 us
  Pallas kernels  88.4 us (92%)
  local copies, waits for them, and re-layouts  6.89 us (7%)
    pallas_call x1, Pallas kernels, body(): pl.pallas_call(functools.partial(kernel, tables, cols, width, place_count...  88.4 us
    unnamed x14, local copies, waits for them, and re-layouts  6.89 us

profile of v1, /device:TPU:1, one launch (start us, length us, event | category | flops | bytes accessed | tf_op | source)
XLA Modules:
  0.0 96.0 jit_solution(6762022714935247766)
XLA Ops:
  0.6 0.0 copy-start
  0.6 1.4 %copy-done = bf16[96,32,256]{2,1,0:T(8,128)(2,1)S(1)} copy-done((bf16[96,32,256]{2,1,0:T(8,128)(2,1)S(1)}, bf16[96,32,256]{2,1,0:T(8,128)(2,1)}, u32[]{:S(2)}) %copy-start) | copy-done | bytes 1572888
  2.0 0.0 copy-start.1
  2.0 1.0 %copy-done.1 = s32[96,4,256]{2,1,0:T(4,128)S(1)} copy-done((s32[96,4,256]{2,1,0:T(4,128)S(1)}, s32[96,4,256]{2,1,0:T(4,128)}, u32[]{:S(2)}) %copy-start.1) | copy-done | bytes 393240
  3.0 0.0 copy-start.2
  3.0 0.9 copy-done.2
  4.0 0.0 copy-start.3
  4.0 0.9 copy-done.3
  4.9 0.0 copy-start.4
  4.9 0.7 copy-done.4
  5.6 0.0 copy-start.5
  5.6 0.7 copy-done.5
  6.2 88.4 %shard_map.77 = (f32[2,32,1024]{2,1,0:T(8,128)S(1)}, f32[2,1024]{1,0:T(2,128)S(1)}) custom-call(s32[96]{0:T(128)S(1)} %copy-done.5, bf16[96,32,256]{2,1,0:T(8,128)(2,1)S(1)} %copy-done, s32[96,4,256]{2,1,0:T(4,128)S(1)} %copy-done.1, s32[96,256]{1,0:T(8,128)S(1)} %copy-done.3, f32[2,32,1024]{2,1,0:T(8,128)S(1)} %copy-done.2, f32[2,1024]{1,0:T(2,128)S(1)} %copy-done.4), custom_call_target="tpu_custom_call" | custom-call | flops 3221225472 | bytes 4194304 | tf_op jit(solution)/shard_map/pallas_call | solution.py:252
  94.7 0.7 copy.10
  95.4 0.6 copy.11
Async XLA Ops:
  0.6 1.4 %copy-start = (bf16[96,32,256]{2,1,0:T(8,128)(2,1)S(1)}, bf16[96,32,256]{2,1,0:T(8,128)(2,1)}, u32[]{:S(2)}) copy-start(bf16[96,32,256]{2,1,0:T(8,128)(2,1)} %grad_ref.1) | copy-start | bytes 4718596
  2.0 1.0 %copy-start.1 = (s32[96,4,256]{2,1,0:T(4,128)S(1)}, s32[96,4,256]{2,1,0:T(4,128)}, u32[]{:S(2)}) copy-start(s32[96,4,256]{2,1,0:T(4,128)} %ids_ref.1) | copy-start | bytes 1179652
  3.0 0.9 copy-start.2
  4.0 0.9 copy-start.3
  4.9 0.7 copy-start.4
  5.6 0.7 copy-start.5

commit v2 on v1

v2 whole, which is shorter than its diff:
```python
import functools

import jax
import jax.numpy as jnp
from jax import lax
from jax.experimental import pallas as pl
from jax.experimental.pallas import tpu as pltpu
from jax.sharding import PartitionSpec as P

MESH = pl.DeviceIdType.MESH
LOW = 256


def kernel(
    tables, cols, place_count, order_hbm, grad_hbm, ids_hbm, len_hbm, w_hbm, state_hbm,
    new_w_ref, new_state_ref,
    order_ref, grad_ref, ids_ref, len_ref, w_ref, state_ref,
    send_grad, recv_grad, send_ids, all_ids, acc, own_square, pair_square, squares,
    in_sem, gs_sem, gr_sem, is_sem, ir_sem, cs_sem, cr_sem, ks_sem, kr_sem, qs_sem, qr_sem,
):
    t = lax.axis_index("table")
    c = lax.axis_index("col")
    slots, dim, rows = w_ref.shape
    samples = grad_ref.shape[2]
    highs = rows // LOW
    across = 4 if tables % 4 == 0 else 1
    deep = tables // across
    shares = tables // cols
    chips = cols // 2
    z, x = t // across, t % across
    y, core = c // 2, c % 2
    mate = (t, y * 2 + (1 - core))

    def wrap(value, size):
        return jnp.where(value >= size, value - size, value)

    def beside(dx, sign):
        return wrap(x + (dx if sign > 0 else across - dx), across)

    def above(q, sign):
        far = (q + 1) // 2
        ahead = (q % 2 == 1) if sign > 0 else (q % 2 == 0)
        return wrap(z + jnp.where(ahead, far, deep - far), deep)

    def each_partner(sign, visit):
        line = [beside(dx, sign) for dx in range(across)]
        for dx in range(1, across):
            visit(z * across + line[dx])

        @pl.loop(0, deep - 1)
        def _(step):
            base = above(step + 1, sign) * across
            for dx in range(across):
                visit(base + line[dx])

    def chip_peer(step):
        return wrap(y + step, chips)

    loads = [
        pltpu.make_async_copy(src, dst, in_sem.at[n])
        for n, (src, dst) in enumerate((
            (order_hbm, order_ref), (grad_hbm, grad_ref), (len_hbm, len_ref),
            (ids_hbm, ids_ref), (w_hbm, w_ref), (state_hbm, state_ref),
        ))
    ]
    for load in loads:
        load.start()

    barrier = pltpu.get_barrier_semaphore()
    pl.semaphore_signal(barrier, inc=1, device_id=mate, device_id_type=MESH)

    @pl.loop(1, chips)
    def _(step):
        pl.semaphore_signal(barrier, inc=1, device_id=(t, chip_peer(step) * 2 + core), device_id_type=MESH)

    loads[0].wait()
    loads[1].wait()

    def greet(target):
        pl.semaphore_signal(barrier, inc=1, device_id=(target, c), device_id_type=MESH)
        for slot in range(slots):
            send_grad[target, slot] = grad_ref[order_ref[slots * target + slot]]

    each_partner(1, greet)
    for slot in range(slots):
        recv_grad[t, slot] = grad_ref[order_ref[slots * t + slot]]

    loads[2].wait()
    loads[3].wait()
    place = lax.broadcasted_iota(jnp.int32, (place_count, samples), 0)

    def ids_target(share):
        return (c - t % cols + cols) % cols + cols * share

    for share in range(shares):
        target = ids_target(share)
        live = []
        for slot in range(slots):
            feature = order_ref[slots * target + slot]
            length = len_ref[pl.ds(feature, 1), :]
            live.append(jnp.where(place < length, ids_ref[feature], -1))
        send_ids[share] = jnp.concatenate(live, axis=0)
    acc[...] = jnp.zeros_like(acc)

    pl.semaphore_wait(barrier, tables - 1 + chips - 1 + 1)

    own_ids = all_ids.at[core, y]

    def ids_copy(share, landing):
        return pltpu.make_async_remote_copy(
            src_ref=send_ids.at[share],
            dst_ref=own_ids.at[landing],
            send_sem=is_sem.at[share],
            recv_sem=ir_sem.at[landing],
            device_id=(ids_target(share), c),
            device_id_type=MESH,
        )

    for share in range(shares):
        @pl.when(ids_target(share) == t)
        def _():
            all_ids[core, y, t // cols] = send_ids[share]

        @pl.when(ids_target(share) != t)
        def _():
            ids_copy(share, t // cols).start()

    def grad_copy(target, source):
        return pltpu.make_async_remote_copy(
            src_ref=send_grad.at[target],
            dst_ref=recv_grad.at[source],
            send_sem=gs_sem.at[target],
            recv_sem=gr_sem.at[source],
            device_id=(target, c),
            device_id_type=MESH,
        )

    each_partner(1, lambda target: grad_copy(target, t).start())

    for share in range(shares):
        @pl.when(ids_target(share) != t)
        def _():
            ids_copy(share, share).wait_recv()

    def chip_ids(peer, owner):
        return pltpu.make_async_remote_copy(
            src_ref=all_ids.at[core, owner],
            dst_ref=all_ids.at[core, owner],
            send_sem=cs_sem.at[peer],
            recv_sem=cr_sem.at[owner],
            device_id=(t, peer * 2 + core),
            device_id_type=MESH,
        )

    @pl.loop(1, chips)
    def _(step):
        chip_ids(chip_peer(step), y).start()

    @pl.loop(1, chips)
    def _(step):
        peer = chip_peer(step)
        chip_ids(peer, peer).wait_recv()

    def mate_ids(owner):
        return pltpu.make_async_remote_copy(
            src_ref=all_ids.at[owner],
            dst_ref=all_ids.at[owner],
            send_sem=ks_sem.at[0],
            recv_sem=kr_sem.at[0],
            device_id=mate,
            device_id_type=MESH,
        )

    mate_ids(core).start()
    mate_ids(1 - core).wait_recv()

    low_line = lax.broadcasted_iota(jnp.int32, (LOW, samples), 0).astype(jnp.float32).astype(jnp.bfloat16)
    one, none = jnp.bfloat16(1.0), jnp.bfloat16(0.0)

    def work(source):
        holder = (source + t) % cols
        block = all_ids[holder % 2, holder // 2, source // cols]
        high = (block >> 8).astype(jnp.float32).astype(jnp.bfloat16)
        low = (block & (LOW - 1)).astype(jnp.float32).astype(jnp.bfloat16)
        for slot in range(slots):
            grad = recv_grad[source, slot]
            left, right = [], []
            for p in range(place_count):
                row = slot * place_count + p
                low_row = jnp.broadcast_to(low[row:row + 1], (LOW, samples))
                right.append(jnp.where(low_row == low_line, one, none))
                high_row = jnp.broadcast_to(high[row:row + 1], (dim, samples))
                left.append(jnp.concatenate(
                    [jnp.where(high_row == jnp.bfloat16(h), grad, none) for h in range(highs)], axis=0))
            acc[slot] += lax.dot_general(
                jnp.concatenate(left, axis=1), jnp.concatenate(right, axis=1),
                (((1,), (1,)), ((), ())), preferred_element_type=jnp.float32)

    work(t)

    @pl.loop(1, tables)
    def _(step):
        turned = jnp.where(step >= tables, step - tables + 1, step)
        q = jnp.where(step >= tables, 0, step // across)
        source = above(q, -1) * across + wrap(x + across - turned % across, across)
        grad_copy(source, source).wait_recv()
        work(source)

    loads[4].wait()
    loads[5].wait()
    sums = []
    for slot in range(slots):
        for h in range(highs):
            part = acc[slot, h * dim:(h + 1) * dim, :]
            sums.append(jnp.sum(part * part, axis=0, keepdims=True))
    own_square[...] = jnp.concatenate(sums, axis=0)

    mate_square = pltpu.make_async_remote_copy(
        src_ref=own_square,
        dst_ref=pair_square,
        send_sem=ks_sem.at[1],
        recv_sem=kr_sem.at[1],
        device_id=mate,
        device_id_type=MESH,
    )
    mate_square.start()
    mate_square.wait_recv()
    squares[y] = own_square[...] + pair_square[...]

    def square_copy(peer, owner):
        return pltpu.make_async_remote_copy(
            src_ref=squares.at[owner],
            dst_ref=squares.at[owner],
            send_sem=qs_sem.at[peer],
            recv_sem=qr_sem.at[owner],
            device_id=(t, peer * 2 + core),
            device_id_type=MESH,
        )

    for step in range(1, chips):
        square_copy(chip_peer(step), y).start()

    for step in range(1, chips):
        peer = chip_peer(step)
        square_copy(peer, peer).wait_recv()

    total = squares[0]
    for peer in range(1, chips):
        total = total + squares[peer]
    full = dim * cols
    for slot in range(slots):
        for h in range(highs):
            row = slot * highs + h
            span = slice(h * LOW, (h + 1) * LOW)
            new_state = state_ref[slot:slot + 1, span] + total[row:row + 1] / full
            new_state_ref[slot:slot + 1, span] = new_state
            scale = 0.3 / jnp.sqrt(new_state)
            new_w_ref[slot, :, span] = w_ref[slot, :, span] - acc[slot, h * dim:(h + 1) * dim, :] * scale

    for share in range(shares):
        @pl.when(ids_target(share) != t)
        def _():
            ids_copy(share, t // cols).wait_send()

    mate_ids(core).wait_send()
    mate_square.wait_send()

    @pl.loop(1, chips)
    def _(step):
        peer = chip_peer(step)
        chip_ids(peer, y).wait_send()
        square_copy(peer, y).wait_send()

    each_partner(1, lambda target: grad_copy(target, t).wait_send())


def solution(mesh):
    tables, cols = mesh.shape["table"], mesh.shape["col"]

    def body(pooled_grad, row_ids, lengths, feature_order, weights, state):
        features, width, samples = pooled_grad.shape
        place_count = row_ids.shape[1]
        slots, dim, rows = weights.shape
        shares = tables // cols
        vmem = pl.BlockSpec(memory_space=pltpu.VMEM)
        dma = pltpu.SemaphoreType.DMA
        chips = cols // 2
        block = slots * place_count
        squares = (slots * (rows // LOW), LOW)
        return pl.pallas_call(
            functools.partial(kernel, tables, cols, place_count),
            out_shape=(
                jax.ShapeDtypeStruct(weights.shape, jnp.float32),
                jax.ShapeDtypeStruct(state.shape, jnp.float32),
            ),
            in_specs=[pl.BlockSpec(memory_space=pltpu.HBM)] * 6,
            out_specs=(vmem, vmem),
            scratch_shapes=[
                pltpu.SMEM(feature_order.shape, jnp.int32),
                pltpu.VMEM(pooled_grad.shape, jnp.bfloat16),
                pltpu.VMEM(row_ids.shape, jnp.int32),
                pltpu.VMEM(lengths.shape, jnp.int32),
                pltpu.VMEM(weights.shape, jnp.float32),
                pltpu.VMEM(state.shape, jnp.float32),
                pltpu.VMEM((tables, slots, dim, samples), jnp.bfloat16),
                pltpu.VMEM((tables, slots, dim, samples), jnp.bfloat16),
                pltpu.VMEM((shares, block, samples), jnp.int32),
                pltpu.VMEM((2, chips, shares, block, samples), jnp.int32),
                pltpu.VMEM((slots, rows // LOW * dim, LOW), jnp.float32),
                pltpu.VMEM(squares, jnp.float32),
                pltpu.VMEM(squares, jnp.float32),
                pltpu.VMEM((chips,) + squares, jnp.float32),
                dma((6,)),
                dma((tables,)), dma((tables,)),
                dma((shares,)), dma((shares,)),
                dma((chips,)), dma((chips,)),
                dma((2,)), dma((2,)),
                dma((chips,)), dma((chips,)),
            ],
            compiler_params=pltpu.CompilerParams(
                collective_id=0, has_side_effects=True, vmem_limit_bytes=60 * 1024 * 1024
            ),
            cost_estimate=pl.CostEstimate(
                flops=4 * slots * tables * samples * rows * dim, bytes_accessed=4 * 1024 * 1024, transcendentals=0
            ),
        )(feature_order, pooled_grad, row_ids, lengths, weights, state)

    return jax.shard_map(
        body,
        mesh=mesh,
        in_specs=(
            P(None, "col", "table"),
            P(None, None, "table"),
            P(None, "table"),
            P(),
            P("table", "col", None),
            P("table", None),
        ),
        out_specs=(P("table", "col", None), P("table", None)),
        check_vma=False,
    )
```

time: 96.3 us -> 91.2 us (0.947)
  local copies, waits for them, and re-layouts: 6.89 us -> 2.97 us
  Pallas kernels: 88.4 us -> 87.4 us
    unnamed x14 -> x2, local copies, waits for them, and re-layouts: 6.89 us -> 2.97 us
    pallas_call x1, Pallas kernels: 88.4 us -> 87.4 us  [body(): pl.pallas_call(functools.partial(kernel, tables, cols, place_count), out_...]
where the time goes in v2:
time: 91.2 us; the launch traced here: 91 us
  Pallas kernels  87.4 us (96%)
  local copies, waits for them, and re-layouts  2.97 us (3%)
    pallas_call x1, Pallas kernels, body(): pl.pallas_call(functools.partial(kernel, tables, cols, place_count), out_...  87.4 us
    unnamed x2, local copies, waits for them, and re-layouts  2.97 us

profile of v2, /device:TPU:1, one launch (start us, length us, event | category | flops | bytes accessed | tf_op | source)
XLA Modules:
  0.0 91.0 jit_solution(4665441623485304003)
XLA Ops:
  0.6 87.4 %shard_map.77 = (f32[2,32,1024]{2,1,0:T(8,128)}, f32[2,1024]{1,0:T(2,128)}) custom-call(s32[96]{0:T(128)} %order_hbm.1, bf16[96,32,256]{2,1,0:T(8,128)(2,1)} %grad_hbm.1, s32[96,4,256]{2,1,0:T(4,128)} %ids_hbm.1, s32[96,256]{1,0:T(8,128)} %len_hbm.1, f32[2,32,1024]{2,1,0:T(8,128)} %w_hbm.1, f32[2,1024]{1,0:T(2,128)} %state_hbm.1), custom_call_target="tpu_custom_call" | custom-call | flops 3221225472 | bytes 4194304 | tf_op jit(solution)/shard_map/pallas_call | solution.py:290
  88.0 1.7 %copy.10 = f32[2,32,1024]{2,1,0:T(8,128)} copy(f32[2,32,1024]{2,1,0:T(8,128)} %get-tuple-element.4) | data formatting | bytes 524288
  89.7 1.3 %copy.11 = f32[2,1024]{1,0:T(2,128)} copy(f32[2,1024]{1,0:T(2,128)} %get-tuple-element.5) | data formatting | bytes 16384

commit v3 on v2

v3 whole, which is shorter than its diff:
```python
import functools

import jax
import jax.numpy as jnp
from jax import lax
from jax.experimental import pallas as pl
from jax.experimental.pallas import tpu as pltpu
from jax.sharding import PartitionSpec as P

MESH = pl.DeviceIdType.MESH
LOW = 256
DEEP = 12
REACH = 4
STEP = 2


def kernel(
    tables, cols, place_count, order_hbm, grad_hbm, ids_hbm, len_hbm, w_hbm, state_hbm,
    new_w_ref, new_state_ref,
    order_ref, grad_ref, ids_ref, len_ref, w_ref, state_ref,
    send_grad, recv_grad, send_ids, all_ids, acc, partial, own_square, pair_square, squares,
    in_sem, gs_sem, gr_sem, is_sem, ir_sem, cs_sem, cr_sem, ks_sem, kr_sem, qs_sem, qr_sem, ps_sem, pr_sem,
):
    t = lax.axis_index("table")
    c = lax.axis_index("col")
    slots, dim, rows = w_ref.shape
    samples = grad_ref.shape[2]
    highs = rows // LOW
    deep = DEEP
    across = tables // deep
    shares = tables // cols
    chips = cols // 2
    far_blocks = 9 * across
    z, x = t // across, t % across
    y, core = c // 2, c % 2
    mate = (t, y * 2 + (1 - core))

    def wrap(value, size):
        return jnp.where(value >= size, value - size, jnp.where(value < 0, value + size, value))

    def route(block):
        q, dx = block // across, block % across
        ahead = jnp.where(q == 0, dx % 2 == 0, q % 2 == 1)
        far = q <= 8
        reach = jnp.where(q == 0, 4, jnp.where(far, (8 - q) // 2, (12 - q) // 2))
        source = jnp.where(ahead, reach, -reach)
        owner = jnp.where(far, jnp.where(ahead, -STEP, STEP), 0)
        role = jnp.where(far, jnp.where(ahead, 1, 2), 0)
        return source, dx, owner, role

    def send_to(block):
        source, dx, owner, _ = route(block)
        home = wrap(x - dx, across)
        at = wrap(z - source, deep)
        return at * across + home, wrap(at + owner, deep) * across + home

    def chip_peer(step):
        return wrap(y + step, chips)

    loads = [
        pltpu.make_async_copy(src, dst, in_sem.at[n])
        for n, (src, dst) in enumerate((
            (order_hbm, order_ref), (grad_hbm, grad_ref), (len_hbm, len_ref),
            (ids_hbm, ids_ref), (w_hbm, w_ref), (state_hbm, state_ref),
        ))
    ]
    for load in loads:
        load.start()

    barrier = pltpu.get_barrier_semaphore()
    pl.semaphore_signal(barrier, inc=1, device_id=mate, device_id_type=MESH)

    @pl.loop(1, chips)
    def _(step):
        pl.semaphore_signal(barrier, inc=1, device_id=(t, chip_peer(step) * 2 + core), device_id_type=MESH)

    for dx in range(1, across):
        pl.semaphore_signal(barrier, inc=1, device_id=(z * across + wrap(x + dx, across), c), device_id_type=MESH)

    @pl.loop(1, 2 * REACH + 1)
    def _(step):
        plane = wrap(z + jnp.where(step > REACH, REACH - step, step), deep) * across
        for dx in range(across):
            pl.semaphore_signal(barrier, inc=1, device_id=(plane + wrap(x + dx, across), c), device_id_type=MESH)

    loads[0].wait()
    loads[1].wait()

    @pl.loop(0, tables)
    def _(block):
        target, owner = send_to(block)

        @pl.when(target == t)
        def _():
            for slot in range(slots):
                recv_grad[slot, block] = grad_ref[order_ref[slots * owner + slot]]

        @pl.when(target != t)
        def _():
            for slot in range(slots):
                send_grad[slot, block] = grad_ref[order_ref[slots * owner + slot]]

    loads[2].wait()
    loads[3].wait()
    place = lax.broadcasted_iota(jnp.int32, (place_count, samples), 0)
    for share in range(shares):
        _, owner = send_to(c + cols * share)
        live = []
        for slot in range(slots):
            feature = order_ref[slots * owner + slot]
            length = len_ref[pl.ds(feature, 1), :]
            live.append(jnp.where(place < length, ids_ref[feature], -1))
        send_ids[share] = jnp.concatenate(live, axis=0)
    acc[...] = jnp.zeros_like(acc)

    pl.semaphore_wait(barrier, (2 * REACH + 1) * across - 1 + chips - 1 + 1)

    def ids_copy(share):
        return pltpu.make_async_remote_copy(
            src_ref=send_ids.at[share],
            dst_ref=all_ids.at[core, y, share],
            send_sem=is_sem.at[share],
            recv_sem=ir_sem.at[share],
            device_id=(send_to(c + cols * share)[0], c),
            device_id_type=MESH,
        )

    def own_share(share):
        return send_to(c + cols * share)[0] == t

    for share in range(shares):
        @pl.when(own_share(share))
        def _():
            all_ids[core, y, share] = send_ids[share]

        @pl.when(jnp.logical_not(own_share(share)))
        def _():
            ids_copy(share).start()

    def grad_copy(slot, block, target):
        return pltpu.make_async_remote_copy(
            src_ref=send_grad.at[slot, block],
            dst_ref=recv_grad.at[slot, block],
            send_sem=gs_sem.at[slot, block],
            recv_sem=gr_sem.at[slot, block],
            device_id=(target, c),
            device_id_type=MESH,
        )

    def send_blocks(slot, first, last):
        @pl.loop(first, last)
        def _(block):
            target, _ = send_to(block)

            @pl.when(target != t)
            def _():
                grad_copy(slot, block, target).start()

    for slot in range(slots):
        send_blocks(slot, 0, far_blocks)
    for slot in range(slots):
        send_blocks(slot, far_blocks, tables)

    for share in range(shares):
        @pl.when(jnp.logical_not(own_share(share)))
        def _():
            ids_copy(share).wait_recv()

    def chip_ids(peer, owner):
        return pltpu.make_async_remote_copy(
            src_ref=all_ids.at[core, owner],
            dst_ref=all_ids.at[core, owner],
            send_sem=cs_sem.at[peer],
            recv_sem=cr_sem.at[owner],
            device_id=(t, peer * 2 + core),
            device_id_type=MESH,
        )

    @pl.loop(1, chips)
    def _(step):
        chip_ids(chip_peer(step), y).start()

    @pl.loop(1, chips)
    def _(step):
        peer = chip_peer(step)
        chip_ids(peer, peer).wait_recv()

    def mate_ids(owner):
        return pltpu.make_async_remote_copy(
            src_ref=all_ids.at[owner],
            dst_ref=all_ids.at[owner],
            send_sem=ks_sem.at[0],
            recv_sem=kr_sem.at[0],
            device_id=mate,
            device_id_type=MESH,
        )

    mate_ids(core).start()
    mate_ids(1 - core).wait_recv()

    low_line = lax.broadcasted_iota(jnp.int32, (LOW, samples), 0).astype(jnp.float32).astype(jnp.bfloat16)
    one, none = jnp.bfloat16(1.0), jnp.bfloat16(0.0)

    def work(slot, blocks):
        left, right = [], []
        for block in blocks:
            holder = block % cols
            ids = all_ids[holder % 2, holder // 2, block // cols]
            high = (ids >> 8).astype(jnp.float32).astype(jnp.bfloat16)
            low = (ids & (LOW - 1)).astype(jnp.float32).astype(jnp.bfloat16)
            grad = recv_grad[slot, block]
            for p in range(place_count):
                row = slot * place_count + p
                low_row = jnp.broadcast_to(low[row:row + 1], (LOW, samples))
                right.append(jnp.where(low_row == low_line, one, none))
                high_row = jnp.broadcast_to(high[row:row + 1], (dim, samples))
                left.append(jnp.concatenate(
                    [jnp.where(high_row == jnp.bfloat16(h), grad, none) for h in range(highs)], axis=0))
        role = route(blocks[0])[3]
        acc[role, slot] += lax.dot_general(
            jnp.concatenate(left, axis=1), jnp.concatenate(right, axis=1),
            (((1,), (1,)), ((), ())), preferred_element_type=jnp.float32)

    groups = [(0, 2), (1, 3)] if across == 4 else [(dx,) for dx in range(across)]

    def work_blocks(slot, first, last):
        @pl.loop(first // across, last // across)
        def _(q):
            for group in groups:
                blocks = [q * across + dx for dx in group]
                for block in blocks:
                    target, _ = send_to(block)

                    @pl.when(target != t)
                    def _():
                        grad_copy(slot, block, target).wait_recv()
                work(slot, blocks)

    def partial_copy(slot, side):
        return pltpu.make_async_remote_copy(
            src_ref=acc.at[1 + side, slot],
            dst_ref=partial.at[side, slot],
            send_sem=ps_sem.at[side, slot],
            recv_sem=pr_sem.at[side, slot],
            device_id=(wrap(z + (STEP if side else -STEP), deep) * across + x, c),
            device_id_type=MESH,
        )

    for slot in range(slots):
        work_blocks(slot, 0, far_blocks)
        for side in range(2):
            partial_copy(slot, side).start()
    for slot in range(slots):
        work_blocks(slot, far_blocks, tables)

    loads[4].wait()
    loads[5].wait()
    sums = []
    for slot in range(slots):
        for side in range(2):
            partial_copy(slot, side).wait_recv()
        for h in range(highs):
            part = slice(h * dim, (h + 1) * dim)
            total = acc[0, slot, part, :] + partial[0, slot, part, :] + partial[1, slot, part, :]
            acc[0, slot, part, :] = total
            sums.append(jnp.sum(total * total, axis=0, keepdims=True))
    own_square[...] = jnp.concatenate(sums, axis=0)

    mate_square = pltpu.make_async_remote_copy(
        src_ref=own_square,
        dst_ref=pair_square,
        send_sem=ks_sem.at[1],
        recv_sem=kr_sem.at[1],
        device_id=mate,
        device_id_type=MESH,
    )
    mate_square.start()
    mate_square.wait_recv()
    squares[y] = own_square[...] + pair_square[...]

    def square_copy(peer, owner):
        return pltpu.make_async_remote_copy(
            src_ref=squares.at[owner],
            dst_ref=squares.at[owner],
            send_sem=qs_sem.at[peer],
            recv_sem=qr_sem.at[owner],
            device_id=(t, peer * 2 + core),
            device_id_type=MESH,
        )

    for step in range(1, chips):
        square_copy(chip_peer(step), y).start()

    for step in range(1, chips):
        peer = chip_peer(step)
        square_copy(peer, peer).wait_recv()

    total = squares[0]
    for peer in range(1, chips):
        total = total + squares[peer]
    full = dim * cols
    for slot in range(slots):
        for h in range(highs):
            row = slot * highs + h
            span = slice(h * LOW, (h + 1) * LOW)
            new_state = state_ref[slot:slot + 1, span] + total[row:row + 1] / full
            new_state_ref[slot:slot + 1, span] = new_state
            scale = 0.3 / jnp.sqrt(new_state)
            new_w_ref[slot, :, span] = w_ref[slot, :, span] - acc[0, slot, h * dim:(h + 1) * dim, :] * scale

    for share in range(shares):
        @pl.when(jnp.logical_not(own_share(share)))
        def _():
            ids_copy(share).wait_send()

    mate_ids(core).wait_send()
    mate_square.wait_send()

    @pl.loop(1, chips)
    def _(step):
        peer = chip_peer(step)
        chip_ids(peer, y).wait_send()
        square_copy(peer, y).wait_send()

    for slot in range(slots):
        for side in range(2):
            partial_copy(slot, side).wait_send()

    @pl.loop(0, tables)
    def _(block):
        target, _ = send_to(block)

        @pl.when(target != t)
        def _():
            for slot in range(slots):
                grad_copy(slot, block, target).wait_send()


def solution(mesh):
    tables, cols = mesh.shape["table"], mesh.shape["col"]

    def body(pooled_grad, row_ids, lengths, feature_order, weights, state):
        features, width, samples = pooled_grad.shape
        place_count = row_ids.shape[1]
        slots, dim, rows = weights.shape
        shares = tables // cols
        vmem = pl.BlockSpec(memory_space=pltpu.VMEM)
        dma = pltpu.SemaphoreType.DMA
        chips = cols // 2
        block = slots * place_count
        squares = (slots * (rows // LOW), LOW)
        return pl.pallas_call(
            functools.partial(kernel, tables, cols, place_count),
            out_shape=(
                jax.ShapeDtypeStruct(weights.shape, jnp.float32),
                jax.ShapeDtypeStruct(state.shape, jnp.float32),
            ),
            in_specs=[pl.BlockSpec(memory_space=pltpu.HBM)] * 6,
            out_specs=(vmem, vmem),
            scratch_shapes=[
                pltpu.SMEM(feature_order.shape, jnp.int32),
                pltpu.VMEM(pooled_grad.shape, jnp.bfloat16),
                pltpu.VMEM(row_ids.shape, jnp.int32),
                pltpu.VMEM(lengths.shape, jnp.int32),
                pltpu.VMEM(weights.shape, jnp.float32),
                pltpu.VMEM(state.shape, jnp.float32),
                pltpu.VMEM((slots, tables, dim, samples), jnp.bfloat16),
                pltpu.VMEM((slots, tables, dim, samples), jnp.bfloat16),
                pltpu.VMEM((shares, block, samples), jnp.int32),
                pltpu.VMEM((2, chips, shares, block, samples), jnp.int32),
                pltpu.VMEM((3, slots, rows // LOW * dim, LOW), jnp.float32),
                pltpu.VMEM((2, slots, rows // LOW * dim, LOW), jnp.float32),
                pltpu.VMEM(squares, jnp.float32),
                pltpu.VMEM(squares, jnp.float32),
                pltpu.VMEM((chips,) + squares, jnp.float32),
                dma((6,)),
                dma((slots, tables)), dma((slots, tables)),
                dma((shares,)), dma((shares,)),
                dma((chips,)), dma((chips,)),
                dma((2,)), dma((2,)),
                dma((chips,)), dma((chips,)),
                dma((2, slots)), dma((2, slots)),
            ],
            compiler_params=pltpu.CompilerParams(
                collective_id=0, has_side_effects=True, vmem_limit_bytes=60 * 1024 * 1024
            ),
            cost_estimate=pl.CostEstimate(
                flops=4 * slots * tables * samples * rows * dim, bytes_accessed=4 * 1024 * 1024, transcendentals=0
            ),
        )(feature_order, pooled_grad, row_ids, lengths, weights, state)

    return jax.shard_map(
        body,
        mesh=mesh,
        in_specs=(
            P(None, "col", "table"),
            P(None, None, "table"),
            P(None, "table"),
            P(),
            P("table", "col", None),
            P("table", None),
        ),
        out_specs=(P("table", "col", None), P("table", None)),
        check_vma=False,
    )
```

time: 91.2 us -> 82.9 us (0.909)
  Pallas kernels: 87.4 us -> 78.7 us
    pallas_call x1, Pallas kernels: 87.4 us -> 78.7 us  [body(): pl.pallas_call(functools.partial(kernel, tables, cols, place_count), out_...]
where the time goes in v3:
time: 82.9 us; the launch traced here: 82.3 us
  Pallas kernels  78.7 us (95%)
  local copies, waits for them, and re-layouts  2.97 us (4%)
    pallas_call x1, Pallas kernels, body(): pl.pallas_call(functools.partial(kernel, tables, cols, place_count), out_...  78.7 us
    unnamed x2, local copies, waits for them, and re-layouts  2.97 us

profile of v3, /device:TPU:1, one launch (start us, length us, event | category | flops | bytes accessed | tf_op | source)
XLA Modules:
  0.0 82.3 jit_solution(10832492081684357204)
XLA Ops:
  0.6 78.7 %shard_map.77 = (f32[2,32,1024]{2,1,0:T(8,128)}, f32[2,1024]{1,0:T(2,128)}) custom-call(s32[96]{0:T(128)} %order_hbm.1, bf16[96,32,256]{2,1,0:T(8,128)(2,1)} %grad_hbm.1, s32[96,4,256]{2,1,0:T(4,128)} %ids_hbm.1, s32[96,256]{1,0:T(8,128)} %len_hbm.1, f32[2,32,1024]{2,1,0:T(8,128)} %w_hbm.1, f32[2,1024]{1,0:T(2,128)} %state_hbm.1), custom_call_target="tpu_custom_call" | custom-call | flops 3221225472 | bytes 4194304 | tf_op jit(solution)/shard_map/pallas_call | solution.py:352
  79.3 1.7 %copy.10 = f32[2,32,1024]{2,1,0:T(8,128)} copy(f32[2,32,1024]{2,1,0:T(8,128)} %get-tuple-element.4) | data formatting | bytes 524288
  81.0 1.3 %copy.11 = f32[2,1024]{1,0:T(2,128)} copy(f32[2,1024]{1,0:T(2,128)} %get-tuple-element.5) | data formatting | bytes 16384

commit v4 on v3

--- a/solution.py
+++ b/solution.py
@@ -8,7 +8,7 @@
 from jax.sharding import PartitionSpec as P
 
 MESH = pl.DeviceIdType.MESH
-LOW = 256
+LOW = 128
 DEEP = 12
 REACH = 4
 STEP = 2
@@ -206,7 +206,7 @@
         for block in blocks:
             holder = block % cols
             ids = all_ids[holder % 2, holder // 2, block // cols]
-            high = (ids >> 8).astype(jnp.float32).astype(jnp.bfloat16)
+            high = (ids >> (LOW.bit_length() - 1)).astype(jnp.float32).astype(jnp.bfloat16)
             low = (ids & (LOW - 1)).astype(jnp.float32).astype(jnp.bfloat16)
             grad = recv_grad[slot, block]
             for p in range(place_count):

time: 82.9 us -> 73.9 us (0.89)
  Pallas kernels: 78.7 us -> 70.1 us
    pallas_call x1, Pallas kernels: 78.7 us -> 70.1 us  [body(): pl.pallas_call(functools.partial(kernel, tables, cols, place_count), out_...]
where the time goes in v4:
time: 73.9 us; the launch traced here: 73.7 us
  Pallas kernels  70.1 us (95%)
  local copies, waits for them, and re-layouts  2.97 us (4%)
    pallas_call x1, Pallas kernels, body(): pl.pallas_call(functools.partial(kernel, tables, cols, place_count), out_...  70.1 us
    unnamed x2, local copies, waits for them, and re-layouts  2.97 us

profile of v4, /device:TPU:1, one launch (start us, length us, event | category | flops | bytes accessed | tf_op | source)
XLA Modules:
  0.0 73.7 jit_solution(14036796240081113508)
XLA Ops:
  0.6 70.1 %shard_map.77 = (f32[2,32,1024]{2,1,0:T(8,128)}, f32[2,1024]{1,0:T(2,128)}) custom-call(s32[96]{0:T(128)} %order_hbm.1, bf16[96,32,256]{2,1,0:T(8,128)(2,1)} %grad_hbm.1, s32[96,4,256]{2,1,0:T(4,128)} %ids_hbm.1, s32[96,256]{1,0:T(8,128)} %len_hbm.1, f32[2,32,1024]{2,1,0:T(8,128)} %w_hbm.1, f32[2,1024]{1,0:T(2,128)} %state_hbm.1), custom_call_target="tpu_custom_call" | custom-call | flops 3221225472 | bytes 4194304 | tf_op jit(solution)/shard_map/pallas_call | solution.py:352
  70.7 1.7 %copy.10 = f32[2,32,1024]{2,1,0:T(8,128)} copy(f32[2,32,1024]{2,1,0:T(8,128)} %get-tuple-element.4) | data formatting | bytes 524288
  72.4 1.3 %copy.11 = f32[2,1024]{1,0:T(2,128)} copy(f32[2,1024]{1,0:T(2,128)} %get-tuple-element.5) | data formatting | bytes 16384

commit v5 on v4

--- a/solution.py
+++ b/solution.py
@@ -68,7 +68,13 @@
         load.start()
 
     barrier = pltpu.get_barrier_semaphore()
-    pl.semaphore_signal(barrier, inc=1, device_id=mate, device_id_type=MESH)
+
+    @pl.loop(0, 2 * REACH)
+    def _(step):
+        away = REACH - step // 2
+        plane = wrap(z + jnp.where(step % 2 == 0, away, -away), deep) * across
+        for dx in range(across):
+            pl.semaphore_signal(barrier, inc=1, device_id=(plane + wrap(x + dx, across), c), device_id_type=MESH)
 
     @pl.loop(1, chips)
     def _(step):
@@ -76,12 +82,7 @@
 
     for dx in range(1, across):
         pl.semaphore_signal(barrier, inc=1, device_id=(z * across + wrap(x + dx, across), c), device_id_type=MESH)
-
-    @pl.loop(1, 2 * REACH + 1)
-    def _(step):
-        plane = wrap(z + jnp.where(step > REACH, REACH - step, step), deep) * across
-        for dx in range(across):
-            pl.semaphore_signal(barrier, inc=1, device_id=(plane + wrap(x + dx, across), c), device_id_type=MESH)
+    pl.semaphore_signal(barrier, inc=1, device_id=mate, device_id_type=MESH)
 
     loads[0].wait()
     loads[1].wait()

time: 73.9 us -> 73.4 us (level)
  no operation moved by 1% of the time
where the time goes in v5:
time: 73.4 us; the launch traced here: 73.1 us
  Pallas kernels  69.5 us (95%)
  local copies, waits for them, and re-layouts  2.97 us (4%)
    pallas_call x1, Pallas kernels, body(): pl.pallas_call(functools.partial(kernel, tables, cols, place_count), out_...  69.5 us
    unnamed x2, local copies, waits for them, and re-layouts  2.97 us

profile of v5, /device:TPU:1, one launch (start us, length us, event | category | flops | bytes accessed | tf_op | source)
XLA Modules:
  0.0 73.1 jit_solution(13420517766724008765)
XLA Ops:
  0.6 69.5 %shard_map.77 = (f32[2,32,1024]{2,1,0:T(8,128)}, f32[2,1024]{1,0:T(2,128)}) custom-call(s32[96]{0:T(128)} %order_hbm.1, bf16[96,32,256]{2,1,0:T(8,128)(2,1)} %grad_hbm.1, s32[96,4,256]{2,1,0:T(4,128)} %ids_hbm.1, s32[96,256]{1,0:T(8,128)} %len_hbm.1, f32[2,32,1024]{2,1,0:T(8,128)} %w_hbm.1, f32[2,1024]{1,0:T(2,128)} %state_hbm.1), custom_call_target="tpu_custom_call" | custom-call | flops 3221225472 | bytes 4194304 | tf_op jit(solution)/shard_map/pallas_call | solution.py:353
  70.2 1.7 %copy.10 = f32[2,32,1024]{2,1,0:T(8,128)} copy(f32[2,32,1024]{2,1,0:T(8,128)} %get-tuple-element.4) | data formatting | bytes 524288
  71.8 1.3 %copy.11 = f32[2,1024]{1,0:T(2,128)} copy(f32[2,1024]{1,0:T(2,128)} %get-tuple-element.5) | data formatting | bytes 16384

commit v6 on v5

--- a/solution.py
+++ b/solution.py
@@ -289,7 +289,7 @@
             device_id_type=MESH,
         )
 
-    for step in range(1, chips):
+    for step in sorted(range(1, chips), key=lambda step: -min(step, chips - step)):
         square_copy(chip_peer(step), y).start()
 
     for step in range(1, chips):

time: 73.4 us -> 73.5 us (level)
  no operation moved by 1% of the time
where the time goes in v6:
time: 73.5 us; the launch traced here: 73.2 us
  Pallas kernels  69.6 us (95%)
  local copies, waits for them, and re-layouts  2.97 us (4%)
    pallas_call x1, Pallas kernels, body(): pl.pallas_call(functools.partial(kernel, tables, cols, place_count), out_...  69.6 us
    unnamed x2, local copies, waits for them, and re-layouts  2.97 us

profile of v6, /device:TPU:1, one launch (start us, length us, event | category | flops | bytes accessed | tf_op | source)
XLA Modules:
  0.0 73.2 jit_solution(12685268982092483642)
XLA Ops:
  0.6 69.6 %shard_map.77 = (f32[2,32,1024]{2,1,0:T(8,128)}, f32[2,1024]{1,0:T(2,128)}) custom-call(s32[96]{0:T(128)} %order_hbm.1, bf16[96,32,256]{2,1,0:T(8,128)(2,1)} %grad_hbm.1, s32[96,4,256]{2,1,0:T(4,128)} %ids_hbm.1, s32[96,256]{1,0:T(8,128)} %len_hbm.1, f32[2,32,1024]{2,1,0:T(8,128)} %w_hbm.1, f32[2,1024]{1,0:T(2,128)} %state_hbm.1), custom_call_target="tpu_custom_call" | custom-call | flops 3221225472 | bytes 4194304 | tf_op jit(solution)/shard_map/pallas_call | solution.py:353
  70.3 1.7 %copy.10 = f32[2,32,1024]{2,1,0:T(8,128)} copy(f32[2,32,1024]{2,1,0:T(8,128)} %get-tuple-element.4) | data formatting | bytes 524288
  72.0 1.3 %copy.11 = f32[2,1024]{1,0:T(2,128)} copy(f32[2,1024]{1,0:T(2,128)} %get-tuple-element.5) | data formatting | bytes 16384
